TPU v7x, 256 devices: a whole 4x4x8 slice. The times are simulated.
256 devices in a mesh: row: 16 (over x_lo, z), col: 16 (over x_hi, y, core).
Axes of the slice: x: 4 (x_hi: 2, x_lo: 2; x = x_hi * 2 + x_lo), y: 4, z: 8, core: 2. Of those that a mesh axis runs over, the one named last changes fastest.
Arguments:
- points: bfloat16 [96, 1024, 1024], P('row', 'col')
- targets: bfloat16 [96, 1024, 1000], P('row', 'col'), may hold values from -6 to 6
- coeffs: float32 [96, 1024, 1000], P('row', 'col'), may hold values from -0.25 to 0.25
- block_inverse: float32 [96, 1024, 1024], P('row', 'col')
- block_order: int32 [96], replicated, may hold values from 0 to 95, each once
Outputs:
- coeffs_out: float32 [96, 1024, 1000], P('row', 'col')
All inputs are finite; a program needn't handle non-finite values.
Results may differ from a plain program's by a relative error of at most 0.0003.
Values may be sent and summed in bfloat16 or wider, within the bound.
A program may use at most 64 MiB of HBM per device.

v0:
```python
import jax
import jax.numpy as jnp
from jax import lax
from jax.sharding import PartitionSpec as P

STEPS = 2
ridge_weight = 1.0


def broadcast(value, axis, source):
    kept = jnp.where(lax.axis_index(axis) == source, value, 0).astype(value.dtype)
    return lax.psum(kept, axis)


def on_device(points, targets, coeffs, block_inverse, block_order):
    blocks_here, per_col, features = points.shape
    classes = targets.shape[2]
    my_row = lax.axis_index("row")
    my_col = lax.axis_index("col")
    flat_points = points.reshape(blocks_here * per_col, features)
    flat_wide = flat_points.astype(jnp.float32)
    point_squares = jnp.sum(flat_wide * flat_wide, axis=1)
    current = coeffs
    for sweep_step in range(STEPS):
        block_id = block_order[sweep_step]
        local_index = block_id % blocks_here
        owner_row = block_id // blocks_here
        own_slice = lax.dynamic_index_in_dim(points, local_index, 0, keepdims=False)
        full_block = lax.all_gather(own_slice, "col", axis=0, tiled=True)
        active = broadcast(full_block, "row", owner_row)
        active_wide = active.astype(jnp.float32)
        active_squares = jnp.sum(active_wide * active_wide, axis=1)
        inner = lax.dot_general(
            active, flat_points, (((1,), (1,)), ((), ())), preferred_element_type=jnp.float32
        )
        distance = active_squares[:, None] + point_squares[None, :] - 2.0 * inner
        tile_wide = jnp.exp(-distance * (0.5 / features))
        flat_current = current.reshape(blocks_here * per_col, classes)
        products = jnp.dot(
            tile_wide,
            flat_current,
            precision=lax.Precision.HIGHEST,
            preferred_element_type=jnp.float32,
        )
        summed = lax.psum(products, ("row", "col"))
        own_sum = lax.dynamic_slice_in_dim(summed, my_col * per_col, per_col, 0)
        previous = lax.dynamic_index_in_dim(current, local_index, 0, keepdims=False)
        wanted = lax.dynamic_index_in_dim(targets, local_index, 0, keepdims=False).astype(
            jnp.float32
        )
        residual = wanted - own_sum - ridge_weight * previous
        full_residual = lax.all_gather(residual, "col", axis=0, tiled=True)
        inverse_rows = lax.dynamic_index_in_dim(block_inverse, local_index, 0, keepdims=False)
        increment = jnp.dot(
            inverse_rows,
            full_residual,
            precision=lax.Precision.HIGHEST,
            preferred_element_type=jnp.float32,
        )
        updated = jnp.where(my_row == owner_row, previous + increment, previous)
        current = lax.dynamic_update_index_in_dim(current, updated, local_index, 0)
    return current


def solution(mesh):
    placed = (
        P("row", "col", None),
        P("row", "col", None),
        P("row", "col", None),
        P("row", "col", None),
        P(),
    )
    return jax.shard_map(
        on_device, mesh=mesh, in_specs=placed, out_specs=P("row", "col", None), check_vma=False
    )
```

profile of v0, /device:TPU:1, one launch (start us, length us, event | category | flops | bytes accessed | tf_op | source)
XLA Modules:
  0.0 974.1 jit_solution(10416053570746938592)
XLA Ops:
  6.5 1.5 copy.13
  8.1 0.6 fusion.40
  9.8 1.7 constant_dynamic-slice_fusion.2
  11.5 0.0 all-gather.13.cloned.1.call-update
  11.5 0.0 all-gather.11.cloned.1.call-start
  11.6 0.7 all-gather.11.cloned.1.call-update
  12.3 0.0 all-reduce.9.cloned.1.call-start
  14.6 53.9 %all-gather.13.cloned.1.call-done = bf16[1,1024,1024]{2,1,0:T(8,128)(2,1)} async-done(((bf16[1,64,1024]{2,1,0:T(8,128)(2,1)}), bf16[1,1024,1024]{2,1,0:T(8,128)(2,1)}) %all-gather.13.cloned.1.call-update) | async-done | bytes 2097168 | tf_op jit(solution)/shard_map/all_gather | solution.py:29
  68.5 1.5 select_bitcast_fusion
  69.9 52.7 %all-gather.11.cloned.1.call-done = bf16[1,1024,1024]{2,1,0:T(8,128)(2,1)} async-done(((bf16[1,64,1024]{2,1,0:T(8,128)(2,1)}), bf16[1,1024,1024]{2,1,0:T(8,128)(2,1)}) %all-gather.11.cloned.1.call-update) | async-done | bytes 2097168 | tf_op jit(solution)/shard_map/all_gather | solution.py:29
  122.7 1.4 select_bitcast_fusion.1
  124.1 0.0 all-reduce.5.cloned.1.call-start
  124.2 1.4 multiply_reduce_fusion.2
  125.6 0.1 add.75
  125.6 143.2 %all-reduce.9.cloned.1.call-done = (bf16[1024,1024]{1,0:T(8,128)(2,1)}, bf16[1024,1024]{1,0:T(8,128)(2,1)}) async-done(((bf16[1024,1024]{1,0:T(8,128)(2,1)}, bf16[1024,1024]{1,0:T(8,128)(2,1)}), (bf16[1024,1024]{1,0:T(8,128)(2,1)}, bf16[1024,1024]{1,0:T(8,128)(2,1)})) %all-reduce.9.cloned.1.call-update) | async-done | bytes 4194320 | tf_op jit(solution)/shard_map/psum | solution.py:12
  268.9 2.2 multiply_reduce_fusion.1
  271.1 2.4 fusion.41
  273.5 8.6 fusion.7
  282.1 0.0 all-gather.7.cloned.1.call-start
  282.2 273.4 %all-reduce.5.cloned.1.call-done = f32[1024,1000]{1,0:T(8,128)} async-done(((f32[1024,1000]{1,0:T(8,128)}), f32[1024,1000]{1,0:T(8,128)}) %all-reduce.5.cloned.1.call-update) | async-done | bytes 4096016 | tf_op jit(solution)/shard_map/psum | solution.py:45
  555.6 1.7 fusion.29
  557.3 0.2 all-reduce.7.cloned.1.call-start
  557.6 2.2 multiply_reduce_fusion
  559.8 3.6 fusion.42
  563.4 56.2 %all-gather.7.cloned.1.call-done = f32[1024,1000]{1,0:T(8,128)} async-done(((f32[64,1000]{1,0:T(8,128)}), f32[1024,1000]{1,0:T(8,128)}) %all-gather.7.cloned.1.call-update) | async-done | bytes 4096016 | tf_op jit(solution)/shard_map/all_gather | solution.py:52
  619.6 4.9 fusion.19
  624.6 8.6 fusion
  633.2 0.0 all-gather.9.cloned.1.call-start
  633.3 264.6 %all-reduce.7.cloned.1.call-done = f32[1024,1000]{1,0:T(8,128)} async-done(((f32[1024,1000]{1,0:T(8,128)}), f32[1024,1000]{1,0:T(8,128)}) %all-reduce.7.cloned.1.call-update) | async-done | bytes 4096016 | tf_op jit(solution)/shard_map/psum | solution.py:45
  897.9 1.7 fusion.28
  899.6 62.0 %all-gather.9.cloned.1.call-done = f32[1024,1000]{1,0:T(8,128)} async-done(((f32[64,1000]{1,0:T(8,128)}), f32[1024,1000]{1,0:T(8,128)}) %all-gather.9.cloned.1.call-update) | async-done | bytes 4096016 | tf_op jit(solution)/shard_map/all_gather | solution.py:52
  961.7 5.5 fusion.16
  (20 shorter events, 0.2 us)
Async XLA Ops:
  6.5 613.1 %copy-start = (f32[6,64,1024]{2,1,0:T(8,128)S(1)}, f32[6,64,1024]{2,1,0:T(8,128)}, u32[]{:S(2)}) copy-start(f32[6,64,1024]{2,1,0:T(8,128)} %param.8) | copy-start | bytes 4718596
  6.5 1.5 copy-start.5
  6.5 61.9 %all-gather.13.cloned.1.call-start = ((), (), s32[]{:S(2)}) async-start(), calls=%async_computation.5 | async-start | bytes 2228224 | tf_op jit(solution)/shard_map/all_gather | solution.py:29
  11.5 111.2 %all-gather.11.cloned.1.call-start = ((), (), s32[]{:S(2)}) async-start(), calls=%async_computation.4 | async-start | bytes 2228224 | tf_op jit(solution)/shard_map/all_gather | solution.py:29
  12.3 256.6 %all-reduce.9.cloned.1.call-start = ((), (), s32[]{:S(2)}) async-start(), calls=%async_computation.6 | async-start | bytes 8388608 | tf_op jit(solution)/shard_map/psum | solution.py:12
  124.1 431.4 %all-reduce.5.cloned.1.call-start = ((), (), s32[]{:S(2)}) async-start(), calls=%async_computation | async-start | bytes 8388608 | tf_op jit(solution)/shard_map/psum | solution.py:45
  268.9 2.2 copy-start.3
  282.1 337.5 %all-gather.7.cloned.1.call-start = ((), (), s32[]{:S(2)}) async-start(), calls=%async_computation.1 | async-start | bytes 4456448 | tf_op jit(solution)/shard_map/all_gather | solution.py:52
  557.3 340.5 %all-reduce.7.cloned.1.call-start = ((), (), s32[]{:S(2)}) async-start(), calls=%async_computation.2 | async-start | bytes 8388608 | tf_op jit(solution)/shard_map/psum | solution.py:45
  557.5 2.3 copy-start.2
  619.6 5.0 copy-start.4
  624.6 275.0 %copy-start.1 = (f32[6,64,1000]{2,1,0:T(8,128)}, f32[6,64,1000]{2,1,0:T(8,128)S(1)}, u32[]{:S(2)}) copy-start(f32[6,64,1000]{2,1,0:T(8,128)S(1)} %fusion.19) | copy-start | bytes 4608004
  633.2 328.5 %all-gather.9.cloned.1.call-start = ((), (), s32[]{:S(2)}) async-start(), calls=%async_computation.3 | async-start | bytes 4456448 | tf_op jit(solution)/shard_map/all_gather | solution.py:52
Sparse Core Ops, SparseCore 0:
  11.6 56.7 all-gather.12
  71.2 51.4 all-gather.10
  125.4 143.4 all-reduce.8
  282.3 273.2 all-reduce.4
  558.5 61.0 all-gather.6
  633.3 264.4 all-reduce.6
  900.6 61.0 all-gather.8
where the time goes:
time: 974 us
  waiting for transfers between devices  907 us (93%)
  matrix products  33.7 us (3%)
  between operations  17 us (2%)
  other arithmetic  12.2 us (1%)
    psum x2, waiting for transfers between devices, on_device(): summed = lax.psum(products, ('row', 'col'))  538 us
    psum x1, waiting for transfers between devices, broadcast(): return lax.psum(kept, axis)  143 us
    all_gather x2, waiting for transfers between devices, on_device(): full_residual = lax.all_gather(residual, 'col', axis=0, tiled=True)  118 us
    all_gather x2, waiting for transfers between devices, on_device(): full_block = lax.all_gather(own_slice, 'col', axis=0, tiled=True)  107 us
  transfers between devices with their start and end apart: 7, of which 7 were waited for; matrix products, arithmetic and copies ran while one was open for 1% of the time, Pallas kernels for 0%

commit v1 on v0

--- a/solution.py
+++ b/solution.py
@@ -42,7 +42,9 @@
             precision=lax.Precision.HIGHEST,
             preferred_element_type=jnp.float32,
         )
-        summed = lax.psum(products, ("row", "col"))
+        summed = products
+        for dev_i in ("col", "row"):
+            summed = lax.psum(summed, axis_name=dev_i)
         own_sum = lax.dynamic_slice_in_dim(summed, my_col * per_col, per_col, 0)
         previous = lax.dynamic_index_in_dim(current, local_index, 0, keepdims=False)
         wanted = lax.dynamic_index_in_dim(targets, local_index, 0, keepdims=False).astype(

time: 974 us -> 1060 us (1.088)
  waiting for transfers between devices: 907 us -> 992 us
    psum x2 -> x4, waiting for transfers between devices: 538 us -> 611 us  [on_device(): summed = lax.psum(summed, axis_name=dev_i)]
    all_gather x2, waiting for transfers between devices: 118 us -> 130 us  [on_device(): full_residual = lax.all_gather(residual, 'col', axis=0, tiled=True)]
  transfers between devices with their start and end apart: 7 -> 9, of which waited for: 7 -> 9; matrix products, arithmetic and copies ran while one was open for 1% -> 1% of each run, Pallas kernels for 0% -> 0%
where the time goes in v1:
time: 1060 us
  waiting for transfers between devices  992 us (94%)
  matrix products  33.7 us (3%)
  between operations  16.7 us (2%)
  other arithmetic  12.2 us (1%)
    psum x4, waiting for transfers between devices, on_device(): summed = lax.psum(summed, axis_name=dev_i)  611 us
    psum x1, waiting for transfers between devices, broadcast(): return lax.psum(kept, axis)  143 us
    all_gather x2, waiting for transfers between devices, on_device(): full_residual = lax.all_gather(residual, 'col', axis=0, tiled=True)  130 us
    all_gather x2, waiting for transfers between devices, on_device(): full_block = lax.all_gather(own_slice, 'col', axis=0, tiled=True)  107 us
  transfers between devices with their start and end apart: 9, of which 9 were waited for; matrix products, arithmetic and copies ran while one was open for 1% of the time, Pallas kernels for 0%

profile of v1, /device:TPU:1, one launch (start us, length us, event | category | flops | bytes accessed | tf_op | source)
XLA Modules:
  0.0 1058.9 jit_solution(2426635903485950652)
XLA Ops:
  6.5 1.5 copy.15
  8.1 0.6 fusion.40
  9.8 1.7 constant_dynamic-slice_fusion.2
  11.5 0.0 all-gather.11.cloned.1.call-start
  11.6 0.7 all-gather.11.cloned.1.call-update
  14.6 53.9 %all-gather.13.cloned.1.call-done = bf16[1,1024,1024]{2,1,0:T(8,128)(2,1)} async-done(((bf16[1,64,1024]{2,1,0:T(8,128)(2,1)}), bf16[1,1024,1024]{2,1,0:T(8,128)(2,1)}) %all-gather.13.cloned.1.call-update) | async-done | bytes 2097168 | tf_op jit(solution)/shard_map/all_gather | solution.py:29
  68.5 1.5 select_bitcast_fusion
  69.9 52.7 %all-gather.11.cloned.1.call-done = bf16[1,1024,1024]{2,1,0:T(8,128)(2,1)} async-done(((bf16[1,64,1024]{2,1,0:T(8,128)(2,1)}), bf16[1,1024,1024]{2,1,0:T(8,128)(2,1)}) %all-gather.11.cloned.1.call-update) | async-done | bytes 2097168 | tf_op jit(solution)/shard_map/all_gather | solution.py:29
  122.7 1.4 select_bitcast_fusion.1
  124.1 0.0 all-reduce.7.cloned.1.call-start
  124.2 1.4 multiply_reduce_fusion.2
  125.6 0.1 add.79
  125.6 143.2 %all-reduce.15.cloned.1.call-done = (bf16[1024,1024]{1,0:T(8,128)(2,1)}, bf16[1024,1024]{1,0:T(8,128)(2,1)}) async-done(((bf16[1024,1024]{1,0:T(8,128)(2,1)}, bf16[1024,1024]{1,0:T(8,128)(2,1)}), (bf16[1024,1024]{1,0:T(8,128)(2,1)}, bf16[1024,1024]{1,0:T(8,128)(2,1)})) %all-reduce.15.cloned.1.call-update) | async-done | bytes 4194320 | tf_op jit(solution)/shard_map/psum | solution.py:12
  268.9 2.2 multiply_reduce_fusion.1
  271.1 2.4 fusion.41
  273.5 8.6 fusion.7
  282.1 0.0 all-reduce.9.cloned.1.call-start
  282.2 161.3 %all-reduce.7.cloned.1.call-done = f32[1024,1000]{1,0:T(8,128)} async-done(((f32[1024,1000]{1,0:T(8,128)}), f32[1024,1000]{1,0:T(8,128)}) %all-reduce.7.cloned.1.call-update) | async-done | bytes 4096016 | tf_op jit(solution)/shard_map/psum | solution.py:47
  443.5 148.7 %all-reduce.9.cloned.1.call-done = f32[1024,1000]{1,0:T(8,128)} async-done(((f32[1024,1000]{1,0:T(8,128)}), f32[1024,1000]{1,0:T(8,128)}) %all-reduce.9.cloned.1.call-update) | async-done | bytes 4096016 | tf_op jit(solution)/shard_map/psum | solution.py:47
  592.2 1.7 fusion.29
  593.9 0.2 all-reduce.11.cloned.1.call-start
  594.2 2.2 multiply_reduce_fusion
  596.4 3.6 fusion.42
  600.0 61.9 %all-gather.7.cloned.1.call-done = f32[1024,1000]{1,0:T(8,128)} async-done(((f32[64,1000]{1,0:T(8,128)}), f32[1024,1000]{1,0:T(8,128)}) %all-gather.7.cloned.1.call-update) | async-done | bytes 4096016 | tf_op jit(solution)/shard_map/all_gather | solution.py:54
  661.9 4.9 fusion.19
  666.9 8.6 fusion
  675.5 0.0 all-reduce.13.cloned.1.call-start
  675.5 152.5 %all-reduce.11.cloned.1.call-done = f32[1024,1000]{1,0:T(8,128)} async-done(((f32[1024,1000]{1,0:T(8,128)}), f32[1024,1000]{1,0:T(8,128)}) %all-reduce.11.cloned.1.call-update) | async-done | bytes 4096016 | tf_op jit(solution)/shard_map/psum | solution.py:47
  828.1 149.0 %all-reduce.13.cloned.1.call-done = f32[1024,1000]{1,0:T(8,128)} async-done(((f32[1024,1000]{1,0:T(8,128)}), f32[1024,1000]{1,0:T(8,128)}) %all-reduce.13.cloned.1.call-update) | async-done | bytes 4096016 | tf_op jit(solution)/shard_map/psum | solution.py:47
  977.0 1.7 fusion.28
  978.9 68.0 %all-gather.9.cloned.1.call-done = f32[1024,1000]{1,0:T(8,128)} async-done(((f32[64,1000]{1,0:T(8,128)}), f32[1024,1000]{1,0:T(8,128)}) %all-gather.9.cloned.1.call-update) | async-done | bytes 4096016 | tf_op jit(solution)/shard_map/all_gather | solution.py:54
  1046.9 5.5 fusion.16
  (26 shorter events, 0.3 us)
Async XLA Ops:
  6.5 655.3 %copy-start = (f32[6,64,1024]{2,1,0:T(8,128)S(1)}, f32[6,64,1024]{2,1,0:T(8,128)}, u32[]{:S(2)}) copy-start(f32[6,64,1024]{2,1,0:T(8,128)} %param.8) | copy-start | bytes 4718596
  6.5 1.5 copy-start.5
  6.5 61.9 %all-gather.13.cloned.1.call-start = ((), (), s32[]{:S(2)}) async-start(), calls=%async_computation.7 | async-start | bytes 2228224 | tf_op jit(solution)/shard_map/all_gather | solution.py:29
  11.5 111.2 %all-gather.11.cloned.1.call-start = ((), (), s32[]{:S(2)}) async-start(), calls=%async_computation.6 | async-start | bytes 2228224 | tf_op jit(solution)/shard_map/all_gather | solution.py:29
  12.3 256.6 %all-reduce.15.cloned.1.call-start = ((), (), s32[]{:S(2)}) async-start(), calls=%async_computation.8 | async-start | bytes 8388608 | tf_op jit(solution)/shard_map/psum | solution.py:12
  124.1 319.3 %all-reduce.7.cloned.1.call-start = ((), (), s32[]{:S(2)}) async-start(), calls=%async_computation | async-start | bytes 8388608 | tf_op jit(solution)/shard_map/psum | solution.py:47
  268.9 2.2 copy-start.3
  282.1 310.1 %all-reduce.9.cloned.1.call-start = ((), (), s32[]{:S(2)}) async-start(), calls=%async_computation.1 | async-start | bytes 8388608 | tf_op jit(solution)/shard_map/psum | solution.py:47
  443.5 218.4 %all-gather.7.cloned.1.call-start = ((), (), s32[]{:S(2)}) async-start(), calls=%async_computation.2 | async-start | bytes 4456448 | tf_op jit(solution)/shard_map/all_gather | solution.py:54
  593.9 234.0 %all-reduce.11.cloned.1.call-start = ((), (), s32[]{:S(2)}) async-start(), calls=%async_computation.3 | async-start | bytes 8388608 | tf_op jit(solution)/shard_map/psum | solution.py:47
  594.2 2.3 copy-start.2
  661.9 5.0 copy-start.4
  666.8 312.0 %copy-start.1 = (f32[6,64,1000]{2,1,0:T(8,128)}, f32[6,64,1000]{2,1,0:T(8,128)S(1)}, u32[]{:S(2)}) copy-start(f32[6,64,1000]{2,1,0:T(8,128)S(1)} %fusion.19) | copy-start | bytes 4608004
  675.5 301.6 %all-reduce.13.cloned.1.call-start = ((), (), s32[]{:S(2)}) async-start(), calls=%async_computation.4 | async-start | bytes 8388608 | tf_op jit(solution)/shard_map/psum | solution.py:47
  828.0 218.9 %all-gather.9.cloned.1.call-start = ((), (), s32[]{:S(2)}) async-start(), calls=%async_computation.5 | async-start | bytes 4456448 | tf_op jit(solution)/shard_map/all_gather | solution.py:54
Sparse Core Ops, SparseCore 0:
  11.6 56.7 all-gather.12
  71.2 51.4 all-gather.10
  125.4 143.4 all-reduce.14
  282.3 161.1 all-reduce.6
  446.0 146.2 all-reduce.8
  594.8 67.0 all-gather.6
  675.6 152.3 all-reduce.10
  830.7 146.3 all-reduce.12
  979.8 67.0 all-gather.8
